TPU v7x, 32 devices: a whole 2x2x4 slice. The times are simulated.
32 devices in a mesh: rep: 2 (over x), pool: 8 (over z, y), tp: 2 (over core).
Axes of the slice: x: 2, y: 2, z: 4, core: 2. Of those that a mesh axis runs over, the one named last changes fastest.
Arguments:
- doc_hidden: bfloat16 [8192, 8192], P(('rep', 'pool'), 'tp'), parts along dimension 0, may hold values from -6 to 6
- key_projector: bfloat16 [8192, 1024], P(None, 'tp'), may hold values from -0.0625 to 0.0625
- value_projector: bfloat16 [8192, 1024], P(None, 'tp'), may hold values from -0.0625 to 0.0625
- queries: bfloat16 [256, 8192], P(('rep', 'pool'), 'tp'), parts along dimension 0, may hold values from -136 to 136
- lengths: int32 [256], P('rep'), parts along dimension 0, may hold values from 1024 to 4096, as said below
- page_slots: int32 [512], P('rep'), parts along dimension 0, may hold values from 0 to 255, as said below
- out_weight: bfloat16 [8192, 8192], P('tp', 'pool'), may hold values from -0.5 to 0.5
Outputs:
- kv_cache: bfloat16 [8192, 2, 1024], P(('rep', 'pool'), None, 'tp'), parts along dimension 0
- answer: bfloat16 [256, 8192], P('rep', ('pool', 'tp')), parts along dimension 0
There are 2 independent parts, one for each index of `rep`. A program takes and returns all parts, laid end to end along the dimension named above; an argument that names none is the same for every part. Nothing has to cross between parts.
Inputs may be any that keep to these rules, and one draw needn't show every extreme that they name: `lengths`: each question row reads at least 1024 tokens; some row reads all 4096 and some row exactly 1024. `page_slots`: A permutation of the page numbers. Page p is made by pool index p // 32, and cache slot s belongs to pool index s // 32; at most 5 pages of one pool index go to one pool index, and that many do in every draw.
All inputs are finite; a program needn't handle non-finite values.
Results may differ from a plain program's by a relative error of at most 0.012.
The roundings to bfloat16 on the way count: a program that leaves them out, or rounds other values in their place, can miss the bound.
Values may be sent and summed in bfloat16 or wider, within the bound.
A program may use at most 128 MiB of HBM per device.

v0:
```python
import math

import jax
import jax.numpy as jnp
from jax import lax
from jax.sharding import PartitionSpec as P

HEAD_SIZE = 128


def partial_attention(query_all, kv_rows, positions, lengths):
    tokens = kv_rows.shape[0]
    kv_width = kv_rows.shape[2]
    head_dim = HEAD_SIZE
    heads_kv = kv_width // head_dim
    row_count = query_all.shape[0]
    query_group_width = query_all.shape[1] // kv_width
    inv_root = 1.0 / math.sqrt(head_dim)
    query_heads = query_all.reshape(row_count, heads_kv, query_group_width, head_dim)
    key_heads = kv_rows[:, 0].reshape(tokens, heads_kv, head_dim)
    value_heads = kv_rows[:, 1].reshape(tokens, heads_kv, head_dim)
    scores = (
        jnp.einsum("qgjd,tgd->qgjt", query_heads, key_heads, preferred_element_type=jnp.float32)
        * inv_root
    )
    visible = (positions[None, :] < lengths[:, None])[:, None, None, :]
    largest = jnp.max(jnp.where(visible, scores, -1e30), axis=-1)
    weights = jnp.where(visible, jnp.exp(scores - largest[..., None]), 0.0)
    totals = jnp.sum(weights, axis=-1)
    rounded = weights.astype(jnp.bfloat16)
    weighted = jnp.einsum(
        "qgjt,tgd->qgjd", rounded, value_heads, preferred_element_type=jnp.float32
    )
    return (
        largest.reshape(row_count, -1),
        totals.reshape(row_count, -1),
        weighted.reshape(row_count, heads_kv * query_group_width, head_dim),
    )


def shards(doc_hidden, key_projector, value_projector, queries, lengths, page_slots, out_weight):
    gathered = lax.all_gather(doc_hidden, "tp", axis=1, tiled=True)
    hidden = gathered.astype(jnp.float32)
    normed = (hidden * lax.rsqrt(jnp.mean(hidden * hidden, axis=-1, keepdims=True) + 1e-06)).astype(
        jnp.bfloat16
    )
    document_key_rows = jnp.dot(normed, key_projector, preferred_element_type=jnp.float32).astype(
        jnp.bfloat16
    )
    document_value_rows = jnp.dot(
        normed, value_projector, preferred_element_type=jnp.float32
    ).astype(jnp.bfloat16)
    kv_local = jnp.stack([document_key_rows, document_value_rows], axis=1)
    tok_rows = kv_local.shape[0]
    kv_width = kv_local.shape[2]
    pool_count = lax.axis_size("pool")
    own_index = lax.axis_index("pool")
    total_pages = page_slots.shape[0]
    per_device = total_pages // pool_count
    page_len = tok_rows // per_device
    capacity = per_device // pool_count + 1
    slot_table = page_slots.reshape(pool_count, per_device)
    targets = slot_table // per_device
    local_index = jnp.arange(per_device, dtype=jnp.int32)
    earlier = local_index[None, :] < local_index[:, None]
    ranking = jnp.sum(
        ((targets[:, :, None] == targets[:, None, :]) & earlier[None, :, :]).astype(jnp.int32),
        axis=-1,
    )
    own_targets = lax.dynamic_index_in_dim(targets, own_index, 0, keepdims=False)
    own_ranking = lax.dynamic_index_in_dim(ranking, own_index, 0, keepdims=False)
    position_out = own_targets * capacity + own_ranking
    blocks = kv_local.reshape(per_device, page_len, 2, kv_width)
    outgoing = (
        jnp.zeros((pool_count * capacity, page_len, 2, kv_width), jnp.bfloat16)
        .at[position_out]
        .set(blocks)
    )
    incoming = lax.all_to_all(outgoing, "pool", split_axis=0, concat_axis=0, tiled=True)
    source_index = jnp.arange(pool_count, dtype=jnp.int32)[:, None] * capacity + ranking
    for_me = targets == own_index
    recv_index = jnp.where(for_me, source_index, pool_count * capacity).reshape(-1)
    local_slot = jnp.where(for_me, slot_table - own_index * per_device, per_device).reshape(-1)
    slot_of_recv = (
        jnp.full((pool_count * capacity,), per_device, jnp.int32)
        .at[recv_index]
        .set(local_slot, mode="drop")
    )
    cache_blocks = (
        jnp.zeros((per_device, page_len, 2, kv_width), jnp.bfloat16)
        .at[slot_of_recv]
        .set(incoming, mode="drop")
    )
    kv_cache = cache_blocks.reshape(tok_rows, 2, kv_width)
    query_all = lax.all_gather(queries, "pool", axis=0, tiled=True)
    page_of = (
        jnp.zeros((total_pages,), jnp.int32)
        .at[page_slots]
        .set(jnp.arange(total_pages, dtype=jnp.int32))
    )
    own_pages = lax.dynamic_slice_in_dim(page_of, own_index * per_device, per_device)
    positions = (
        own_pages[:, None] * page_len + jnp.arange(page_len, dtype=jnp.int32)[None, :]
    ).reshape(-1)
    largest, totals, weighted = partial_attention(query_all, kv_cache, positions, lengths)
    part_max, part_tot, part_sum = (
        lax.all_to_all(largest[None], "pool", split_axis=1, concat_axis=0, tiled=True),
        lax.all_to_all(totals[None], "pool", split_axis=1, concat_axis=0, tiled=True),
        lax.all_to_all(weighted[None], "pool", split_axis=1, concat_axis=0, tiled=True),
    )
    overall = jnp.max(part_max, axis=0)
    rescale = jnp.exp(part_max - overall[None])
    merged_tot = jnp.sum(part_tot * rescale, axis=0)
    merged_sum = jnp.sum(part_sum * rescale[..., None], axis=0)
    own_rows = (
        (merged_sum / merged_tot[..., None]).reshape(merged_sum.shape[0], -1).astype(jnp.bfloat16)
    )
    attended = lax.all_gather(own_rows, "pool", axis=0, tiled=True)
    projected = jnp.dot(attended, out_weight, preferred_element_type=jnp.float32)
    answer = lax.psum_scatter(projected.astype(jnp.bfloat16), "tp", scatter_dimension=1, tiled=True)
    return (kv_cache, answer)


def solution(mesh):
    in_specs = (
        P(("rep", "pool"), "tp"),
        P(None, "tp"),
        P(None, "tp"),
        P(("rep", "pool"), "tp"),
        P("rep"),
        P("rep"),
        P("tp", "pool"),
    )
    out_specs = (P(("rep", "pool"), None, "tp"), P("rep", ("pool", "tp")))
    return jax.shard_map(shards, mesh=mesh, in_specs=in_specs, out_specs=out_specs, check_vma=False)
```

profile of v0, /device:TPU:0, one launch (start us, length us, event | category | flops | bytes accessed | tf_op | source)
XLA Modules:
  0.0 265.0 jit_solution(2164733074613047799)
XLA Ops:
  8.7 0.8 reshape.204
  9.8 23.1 %all-gather.4.cloned.1.call-done = bf16[512,8192]{1,0:T(8,128)(2,1)} async-done(((bf16[512,4096]{1,0:T(8,128)(2,1)}), bf16[512,8192]{1,0:T(8,128)(2,1)}) %all-gather.4.cloned.1.call-update) | async-done | bytes 8388624 | tf_op jit(solution)/shard_map/all_gather | solution.py:42
  33.0 5.3 %fusion = f32[512]{0:T(512)S(1)} fusion(bf16[512,8192]{1,0:T(8,128)(2,1)} %all-gather.4.cloned.1.call-done), kind=kLoop, calls=%fused_computation.6 | loop fusion | flops 12582400 | bytes 8390656 | tf_op jit(solution)/shard_map/reduce_sum | solution.py:44
  38.7 7.3 %fusion.20 = bf16[512,512]{1,0:T(8,128)(2,1)S(1)} fusion(bf16[8192,512]{1,0:T(8,128)(2,1)} %param.9, bf16[512,8192]{1,0:T(8,128)(2,1)S(1)} %copy-done.1, f32[512]{0:T(512)S(1)} %add_rsqrt_fusion), kind=kOutput, calls=%fused_computation.24 | convolution fusion | flops 4307812352 | bytes 17303552 | tf_op jit(solution)/shard_map/dot_general | solution.py:50
  46.1 4.5 %fusion.17 = bf16[512,512]{1,0:T(8,128)(2,1)S(1)} fusion(bf16[8192,512]{1,0:T(8,128)(2,1)S(1)} %bitcast.82, bf16[512,8192]{1,0:T(8,128)(2,1)S(1)} %copy-done.1, f32[512]{0:T(512)S(1)} %add_rsqrt_fusion), kind=kOutput, calls=%fused_computation.23 | convolution fusion | flops 4307812352 | bytes 17303552 | tf_op jit(solution)/shard_map/dot_general | solution.py:47
  50.7 1.2 broadcast_in_dim.58
  52.0 4.6 %scatter_fusion = bf16[40,16,2,512]{3,1,2,0:T(8,128)(2,1)} fusion(bf16[40,16,2,512]{3,1,2,0:T(8,128)(2,1)} %broadcast_in_dim.58, s32[32]{0:T(128)S(1)} %fusion.26, bf16[32,16,2,512]{3,1,2,0:T(8,128)(2,1)S(1)} %pad_maximum_fusion), kind=kCustom, calls=%fused_computation.1 | custom fusion | bytes 3145856 | tf_op jit(solution)/shard_map/scatter | solution.py:77
  56.6 5.8 %all-to-all-start = ((bf16[40,16,2,512]{3,1,2,0:T(8,128)(2,1)}), bf16[40,16,2,512]{3,1,2,0:T(8,128)(2,1)}, u32[]{:S(2)}, u32[]{:S(2)}) async-start(bf16[40,16,2,512]{3,1,2,0:T(8,128)(2,1)} %scatter_fusion), calls=%async_computation | async-start | bytes 2621440 | tf_op jit(solution)/shard_map/all_to_all | solution.py:79
  63.1 1.4 scatter_custom_fusion.3
  64.8 1.6 scatter_custom_fusion
  66.5 48.8 %all-gather.6.cloned.1.call-done = bf16[128,4096]{1,0:T(8,128)(2,1)} async-done(((bf16[16,4096]{1,0:T(8,128)(2,1)}), bf16[128,4096]{1,0:T(8,128)(2,1)}) %all-gather.6.cloned.1.call-update) | async-done | bytes 1048592 | tf_op jit(solution)/shard_map/all_gather | solution.py:95
  115.3 1.6 copy.56
  117.1 5.0 %scatter_fusion.1 = bf16[32,16,2,512]{3,1,2,0:T(8,128)(2,1)S(1)} fusion(bf16[32,16,2,512]{3,1,2,0:T(8,128)(2,1)S(1)} %broadcast_in_dim.54, s32[40]{0:T(128)S(1)} %compare_select_fusion.2, bf16[40,16,2,512]{3,1,2,0:T(8,128)(2,1)} %all-to-all-done), kind=kCustom, calls=%fused_computation.2 | custom fusion | bytes 3932320 | tf_op jit(solution)/shard_map/scatter | solution.py:92
  122.2 0.9 fusion.34
  123.1 1.3 copy.55
  124.3 1.4 fusion.2
  125.7 3.2 %copy-done = f32[4,512,128,8]{2,1,3,0:T(8,128)} copy-done((f32[4,512,128,8]{2,1,3,0:T(8,128)}, f32[4,512,128,8]{2,1,3,0:T(8,128)S(1)}, u32[]{:S(2)}) %copy-start) | copy-done | bytes 8388632
  129.0 1.8 fusion.5
  131.4 0.8 reduce
  132.9 3.3 %all-to-all-start.3 = ((f32[8,1,512]{2,1,0:T(1,128)}), f32[8,1,512]{2,1,0:T(1,128)S(1)}, u32[]{:S(2)}, u32[]{:S(2)}) async-start(f32[8,1,512]{2,1,0:T(1,128)} %reshape.250), calls=%async_computation.3 | async-start | bytes 32768 | tf_op jit(solution)/shard_map/all_to_all | solution.py:108
  136.3 1.0 copy.54
  137.4 0.8 reduce.2
  138.9 3.9 %all-to-all-done.3 = f32[8,1,512]{2,1,0:T(1,128)S(1)} async-done(((f32[8,1,512]{2,1,0:T(1,128)}), f32[8,1,512]{2,1,0:T(1,128)S(1)}, u32[]{:S(2)}, u32[]{:S(2)}) %all-to-all-start.3) | async-done | bytes 16416 | tf_op jit(solution)/shard_map/all_to_all | solution.py:108
  142.8 3.3 %all-to-all-start.2 = ((f32[8,1,512]{2,1,0:T(1,128)}), f32[8,1,512]{2,1,0:T(1,128)S(1)}, u32[]{:S(2)}, u32[]{:S(2)}) async-start(f32[8,1,512]{2,1,0:T(1,128)} %reshape.248), calls=%async_computation.2 | async-start | bytes 32768 | tf_op jit(solution)/shard_map/all_to_all | solution.py:107
  146.1 5.3 %fusion.7 = f32[4,128,128,8]{2,1,3,0:T(8,128)S(1)} fusion(bf16[512,4,128,1]{0,2,3,1:T(8,128)(2,1)} %bitcast.72, f32[4,512,128,8]{2,1,3,0:T(8,128)} %copy-done, f32[128,4,8]{0,2,1:T(8,128)S(1)} %get-tuple-element.17, pred[128,512]{0,1:T(8,128)(4,1)S(1)} %broadcast_compare_fusion), kind=kOutput, calls=%fused_computation.15 | convolution fusion | flops 545259520 | bytes 11091968 | tf_op jit(solution)/shard_map/qgjt,tgd->qgjd/dot_general | solution.py:31
  151.4 2.1 copy.60
  153.5 5.9 %all-to-all-start.1 = ((f32[1,128,32,128]{3,2,0,1:T(8,128)}), f32[1,128,32,128]{3,2,0,1:T(8,128)S(1)}, u32[]{:S(2)}, u32[]{:S(2)}) async-start(f32[1,128,32,128]{3,2,0,1:T(8,128)} %copy.60), calls=%async_computation.1 | async-start | bytes 4194304 | tf_op jit(solution)/shard_map/all_to_all | solution.py:109
  161.1 43.5 %all-to-all-done.1 = f32[1,128,32,128]{3,2,0,1:T(8,128)S(1)} async-done(((f32[1,128,32,128]{3,2,0,1:T(8,128)}), f32[1,128,32,128]{3,2,0,1:T(8,128)S(1)}, u32[]{:S(2)}, u32[]{:S(2)}) %all-to-all-start.1) | async-done | bytes 2097184 | tf_op jit(solution)/shard_map/all_to_all | solution.py:109
  206.3 39.3 %all-gather.8.cloned.1.call-done = bf16[128,4096]{1,0:T(8,128)(2,1)} async-done(((bf16[16,4096]{1,0:T(8,128)(2,1)}), bf16[128,4096]{1,0:T(8,128)(2,1)}) %all-gather.8.cloned.1.call-update) | async-done | bytes 1048592 | tf_op jit(solution)/shard_map/all_gather | solution.py:118
  245.5 5.7 %convolution_convert_fusion = bf16[128,1024]{1,0:T(8,128)(2,1)} fusion(bf16[128,4096]{1,0:T(8,128)(2,1)} %all-gather.8.cloned.1.call-done, bf16[4096,1024]{1,0:T(8,128)(2,1)} %param.13), kind=kOutput, calls=%fused_computation.25 | convolution fusion | flops 1073872896 | bytes 9699328 | tf_op jit(solution)/shard_map/dot_general | solution.py:119
  251.3 2.0 copy.63
  253.3 4.3 %reduce-scatter.2.cloned.1.call-done = bf16[128,512]{1,0:T(8,128)(2,1)} async-done(((bf16[128,1024]{1,0:T(8,128)(2,1)}), bf16[128,512]{1,0:T(8,128)(2,1)}) %reduce-scatter.2.cloned.1.call-update) | async-done | bytes 131088 | tf_op jit(solution)/shard_map/reduce_scatter | solution.py:120
  (55 shorter events, 8.4 us)
Async XLA Ops:
  8.0 25.0 %all-gather.4.cloned.1.call-start = ((), (), s32[]{:S(2)}) async-start(), calls=%async_computation.5 | async-start | bytes 12582912 | tf_op jit(solution)/shard_map/all_gather | solution.py:42
  33.0 5.8 %copy-start.1 = (bf16[512,8192]{1,0:T(8,128)(2,1)S(1)}, bf16[512,8192]{1,0:T(8,128)(2,1)}, u32[]{:S(2)}) copy-start(bf16[512,8192]{1,0:T(8,128)(2,1)} %all-gather.4.cloned.1.call-done) | copy-start | bytes 25165828
  33.0 13.1 %slice-start = ((s8[8388608]{0:T(1024)(128)(4,1)}), s8[4194304]{0:T(1024)(128)(4,1)S(1)}, s32[]{:S(2)}) async-start(s8[8388608]{0:T(1024)(128)(4,1)} %bitcast.81), calls=%async_computation.9 | async-start | bytes 8388608
  38.7 7.3 %slice-start.1 = ((s8[8388608]{0:T(1024)(128)(4,1)}), s8[4194304]{0:T(1024)(128)(4,1)S(1)}, s32[]{:S(2)}) async-start(s8[8388608]{0:T(1024)(128)(4,1)} %bitcast.81), calls=%async_computation.10 | async-start | bytes 8388608
  50.6 12.5 %copy-start.2 = (s32[256]{0:T(256)S(1)}, s32[256]{0:T(256)}, u32[]{:S(2)}) copy-start(s32[256]{0:T(256)} %param.12) | copy-start | bytes 3076
  50.6 15.8 %copy-start.3 = (s32[128]{0:T(128)S(1)}, s32[128]{0:T(128)}, u32[]{:S(2)}) copy-start(s32[128]{0:T(128)} %param.11) | copy-start | bytes 1540
  56.6 60.3 %all-to-all-start = ((bf16[40,16,2,512]{3,1,2,0:T(8,128)(2,1)}), bf16[40,16,2,512]{3,1,2,0:T(8,128)(2,1)}, u32[]{:S(2)}, u32[]{:S(2)}) async-start(bf16[40,16,2,512]{3,1,2,0:T(8,128)(2,1)} %scatter_fusion), calls=%async_computation | async-start | bytes 2621440 | tf_op jit(solution)/shard_map/all_to_all | solution.py:79
  62.4 52.9 %all-gather.6.cloned.1.call-start = ((), (), s32[]{:S(2)}) async-start(), calls=%async_computation.6 | async-start | bytes 1179648 | tf_op jit(solution)/shard_map/all_gather | solution.py:95
  125.7 3.2 %copy-start = (f32[4,512,128,8]{2,1,3,0:T(8,128)}, f32[4,512,128,8]{2,1,3,0:T(8,128)S(1)}, u32[]{:S(2)}) copy-start(f32[4,512,128,8]{2,1,3,0:T(8,128)S(1)} %get-tuple-element.18) | copy-start | bytes 25165828
  132.9 9.9 %all-to-all-start.3 = ((f32[8,1,512]{2,1,0:T(1,128)}), f32[8,1,512]{2,1,0:T(1,128)S(1)}, u32[]{:S(2)}, u32[]{:S(2)}) async-start(f32[8,1,512]{2,1,0:T(1,128)} %reshape.250), calls=%async_computation.3 | async-start | bytes 32768 | tf_op jit(solution)/shard_map/all_to_all | solution.py:108
  142.8 10.7 %all-to-all-start.2 = ((f32[8,1,512]{2,1,0:T(1,128)}), f32[8,1,512]{2,1,0:T(1,128)S(1)}, u32[]{:S(2)}, u32[]{:S(2)}) async-start(f32[8,1,512]{2,1,0:T(1,128)} %reshape.248), calls=%async_computation.2 | async-start | bytes 32768 | tf_op jit(solution)/shard_map/all_to_all | solution.py:107
  153.5 51.2 %all-to-all-start.1 = ((f32[1,128,32,128]{3,2,0,1:T(8,128)}), f32[1,128,32,128]{3,2,0,1:T(8,128)S(1)}, u32[]{:S(2)}, u32[]{:S(2)}) async-start(f32[1,128,32,128]{3,2,0,1:T(8,128)} %copy.60), calls=%async_computation.1 | async-start | bytes 4194304 | tf_op jit(solution)/shard_map/all_to_all | solution.py:109
  159.4 86.2 %all-gather.8.cloned.1.call-start = ((), (), s32[]{:S(2)}) async-start(), calls=%async_computation.7 | async-start | bytes 1179648 | tf_op jit(solution)/shard_map/all_gather | solution.py:118
  206.2 51.4 %reduce-scatter.2.cloned.1.call-start = ((), (), s32[]{:S(2)}) async-start(), calls=%async_computation.8 | async-start | bytes 393216 | tf_op jit(solution)/shard_map/reduce_scatter | solution.py:120
Sparse Core Ops, SparseCore 0:
  10.4 22.5 all-gather.3
  251.4 6.1 reduce-scatter.1
Sparse Core Ops, SparseCore 1:
  65.0 50.3 all-gather.5
  206.3 39.2 all-gather.7
where the time goes:
time: 266 us; the launch traced here: 265 us
  waiting for transfers between devices  164 us (62%)
  local copies, waits for them, and re-layouts  30.7 us (12%)
  matrix products  24.2 us (9%)
  starting transfers between devices  18.5 us (7%)
  between operations  15.8 us (6%)
  other arithmetic  11.7 us (4%)
    all_gather x1, waiting for transfers between devices, shards(): query_all = lax.all_gather(queries, 'pool', axis=0, tiled=True)  48.8 us
    all_to_all x1, waiting for transfers between devices, shards(): lax.all_to_all(weighted[None], 'pool', split_axis=1, concat_axis=0, tiled...  43.5 us
    all_gather x1, waiting for transfers between devices, shards(): attended = lax.all_gather(own_rows, 'pool', axis=0, tiled=True)  39.3 us
    all_gather x1, waiting for transfers between devices, shards(): gathered = lax.all_gather(doc_hidden, 'tp', axis=1, tiled=True)  23.1 us
    unnamed x19, local copies, waits for them, and re-layouts  8.7 us
    dot_general x1, matrix products, shards(): jnp.dot(normed, value_projector, preferred_element_type=jnp.float32)  7.3 us
    all_to_all x1, starting transfers between devices, shards(): lax.all_to_all(weighted[None], 'pool', split_axis=1, concat_axis=0, tiled...  5.93 us
    all_to_all x1, starting transfers between devices, shards(): lax.all_to_all(outgoing, 'pool', split_axis=0, concat_axis=0, tiled=True)  5.79 us
  transfers between devices with their start and end apart: 8, of which 6 were waited for; matrix products, arithmetic and copies ran while one was open for 7% of the time, Pallas kernels for 0%

commit v1 on v0

v1 whole, which is shorter than its diff:
```python
import functools
import math

import jax
import jax.numpy as jnp
from jax import lax
from jax.experimental import pallas as pl
from jax.experimental.pallas import tpu as pltpu
from jax.sharding import PartitionSpec as P

HEAD = 128
MESH = pl.DeviceIdType.MESH
F32 = jnp.float32
BF16 = jnp.bfloat16


def iota(shape, dim):
    return lax.broadcasted_iota(jnp.int32, shape, dim)


def kernel(
    n, rows, group, page, per, cap,
    doc, wk, wv, q, lens, slots, ow,
    kv_out, ans,
    x, w, wo, qall, kvb, vt, onehot_in, outb, recvb,
    ol, ml, own_o, own_ml, so, sst, ro, rst, att, amat, psend, precv,
    dsem, dsend, drecv, qsend, qrecv, asend, arecv, ksend, krecv,
    osend, orecv, tsend, trecv, psem,
):
    p = lax.axis_index("pool")
    t = lax.axis_index("tp")
    half = n // 2
    tokens = kvb.shape[0] * page
    heads = vt.shape[0]
    width = group * rows
    kvw = heads * HEAD
    snake = n == 8

    if snake:
        z = p // 2
        pos = z + (p % 2) * (n - 1 - 2 * z)
    else:
        pos = p

    def at(k):
        r = (pos + (k % n)) % n
        if not snake:
            return r
        h = r // half
        return 2 * r + h * (2 * (n - 1 - r) + 1 - 2 * r)

    other = 1 - t
    barrier = pltpu.get_barrier_semaphore()
    for k in range(1, n):
        pl.semaphore_signal(barrier, inc=1, device_id={"pool": at(k)}, device_id_type=MESH)
    pl.semaphore_signal(barrier, inc=1, device_id={"tp": other}, device_id_type=MESH)

    nb = dsend.shape[0]
    brows = tokens // nb
    blk = lambda b: pl.ds(b * brows, brows)
    dloc = [pltpu.make_async_copy(doc.at[blk(b)], x.at[t, blk(b)], dsem.at[b]) for b in range(nb)]
    for c in dloc:
        c.start()
    wc = [
        pltpu.make_async_copy(wk, w.at[:, pl.ds(0, kvw)], dsem.at[nb]),
        pltpu.make_async_copy(wv, w.at[:, pl.ds(kvw, kvw)], dsem.at[nb + 1]),
    ]
    oc = pltpu.make_async_copy(ow, wo, dsem.at[nb + 2])
    for c in wc:
        c.start()

    for g in range(heads):
        parts = [
            q[:, (group * g + j) * HEAD : (group * g + j + 1) * HEAD].astype(F32)
            for j in range(group)
        ]
        qall[p, g] = jnp.concatenate(parts, axis=0).astype(BF16)

    pl.semaphore_wait(barrier, n)

    dex = [
        pltpu.make_async_remote_copy(
            doc.at[blk(b)], x.at[t, blk(b)], dsend.at[b], drecv.at[b],
            device_id={"tp": other}, device_id_type=MESH,
        )
        for b in range(nb)
    ]
    for c in dex:
        c.start()
    oc.start()

    def ring(buf, ssem, rsem, s):
        hh = heads // 2
        a, b = at(-s), at(s)
        if s == half - 1:
            ra, rb = buf.at[a, pl.ds(0, hh)], buf.at[b, pl.ds(hh, heads - hh)]
        else:
            ra, rb = buf.at[a], buf.at[b]
        return (
            pltpu.make_async_remote_copy(
                ra, ra, ssem.at[0, s], rsem.at[0, s],
                device_id={"pool": at(1)}, device_id_type=MESH,
            ),
            pltpu.make_async_remote_copy(
                rb, rb, ssem.at[1, s], rsem.at[1, s],
                device_id={"pool": at(-1)}, device_id_type=MESH,
            ),
        )

    def advance(steps, s):
        if s > 0:
            for c in steps[s - 1]:
                c.wait_recv()
        if s < half:
            for c in steps[s]:
                c.start()

    qring = [ring(qall, qsend, qrecv, s) for s in range(half)]
    advance(qring, 0)

    total = n * per
    shift = per.bit_length() - 1
    srow = jnp.broadcast_to(slots[...], (total, total))
    ir, ic = iota((total, total), 0), iota((total, total), 1)
    scol = jnp.sum(jnp.where(ir == ic, srow, 0).astype(F32), axis=1, keepdims=True).astype(jnp.int32)
    tr, tc = srow >> shift, jnp.broadcast_to(scol >> shift, (total, total))
    same = (tr == tc) & ((ir >> shift) == (ic >> shift)) & (ir < ic)
    rank = jnp.sum(jnp.where(same, 1.0, 0.0), axis=0, keepdims=True)
    pageid = iota((1, total), 1)
    dest = (slots[...] >> shift).astype(F32) * cap + rank
    spread = jnp.where(
        iota((total, tokens), 0) == p * per + iota((total, tokens), 1) // page, 1.0, 0.0
    ).astype(BF16)
    dtok = jnp.dot(
        jnp.broadcast_to(dest, (16, total)).astype(BF16), spread, preferred_element_type=F32
    )[0:1].astype(jnp.int32)
    drow = dtok * page + iota((1, tokens), 1) % page
    origin = (pageid >> shift).astype(F32) * cap + rank
    hit = jnp.broadcast_to(slots[...], (tokens, total)) == p * per + iota((tokens, total), 0) // page
    rpage = jnp.sum(
        jnp.where(hit, jnp.broadcast_to(origin, (tokens, total)), 0.0), axis=1, keepdims=True
    ).astype(jnp.int32)
    rrow = rpage * page + iota((tokens, 1), 0) % page
    moved = n * cap * page
    onehot_in[...] = jnp.where(iota((tokens, moved), 1) == rrow, 1.0, 0.0).astype(BF16)

    feat = x.shape[2]
    cols = 256
    qstep = 1
    for b in range(nb):
        dloc[b].wait()
        dex[b].wait_recv()

        @pl.loop(0, brows // 16)
        def _(i):
            r = pl.ds(pl.multiple_of(b * brows + i * 16, 16), 16)
            ss = jnp.zeros((16, 1), F32)
            for h in range(2):
                v = x[h, r, :].astype(F32)
                ss = ss + jnp.sum(v * v, axis=-1, keepdims=True)
            scale = lax.rsqrt(ss / (2 * feat) + 1e-06)
            for h in range(2):
                x[h, r, :] = (x[h, r, :].astype(F32) * scale).astype(BF16)

        if qstep < half:
            advance(qring, qstep)
            qstep += 1
        if b == 0:
            for c in wc:
                c.wait()

        @pl.loop(0, 2 * kvw // cols)
        def _(i):
            cc = pl.ds(pl.multiple_of(i * cols, cols), cols)
            acc = jnp.dot(x[0, blk(b), :], w[pl.ds(0, feat), cc], preferred_element_type=F32)
            acc += jnp.dot(x[1, blk(b), :], w[pl.ds(feat, feat), cc], preferred_element_type=F32)
            kvb[pl.ds(b * brows // page, brows // page), :, cc] = acc.astype(BF16).reshape(
                brows // page, page, cols
            )

        if qstep < half:
            advance(qring, qstep)
            qstep += 1

    onehot_out = jnp.where(iota((moved, tokens), 0) == drow, 1.0, 0.0).astype(BF16)

    @pl.loop(0, 2 * kvw // cols)
    def _(i):
        cc = pl.ds(pl.multiple_of(i * cols, cols), cols)
        outb[:, :, cc] = (
            jnp.dot(onehot_out, kvb[:, :, cc].reshape(tokens, cols), preferred_element_type=F32)
            .astype(BF16)
            .reshape(n, cap * page, cols)
        )

    recvb[p] = outb[p]
    ksends = [
        pltpu.make_async_remote_copy(
            outb.at[at(k)], recvb.at[p], ksend.at[k - 1], krecv.at[k - 1],
            device_id={"pool": at(k)}, device_id_type=MESH,
        )
        for k in range(1, n)
    ]
    ksends[0].start()

    while qstep <= half:
        advance(qring, qstep)
        qstep += 1

    for g in range(heads):
        vt[g] = (
            kvb[:, :, kvw + g * HEAD : kvw + (g + 1) * HEAD]
            .reshape(tokens, HEAD).astype(F32).T.astype(BF16)
        )

    lr = jnp.broadcast_to(lens[...], (n * rows, n * rows))
    eye = iota((n * rows, n * rows), 0) == iota((n * rows, n * rows), 1)
    lcol = jnp.sum(jnp.where(eye, lr, 0).astype(F32), axis=1, keepdims=True)

    def chunk_lengths(c):
        want = c * rows + iota((n * rows, width), 1) % rows
        pick = jnp.where(iota((n * rows, width), 0) == want, jnp.broadcast_to(lcol, (n * rows, width)), 0.0)
        return jnp.sum(pick, axis=0, keepdims=True).astype(jnp.int32)

    inv_root = 1.0 / math.sqrt(HEAD)

    def attend(ca, cb):
        lim = jnp.concatenate([chunk_lengths(ca), chunk_lengths(cb)], axis=1)
        seen = p * tokens + iota((tokens, 2 * width), 0) < lim

        @pl.loop(0, heads)
        def _(g):
            qq = jnp.concatenate([qall[ca, g], qall[cb, g]], axis=0)
            kk = kvb[:, :, pl.ds(pl.multiple_of(g * HEAD, HEAD), HEAD)].reshape(tokens, HEAD)
            sc = lax.dot_general(kk, qq, (((1,), (1,)), ((), ())), preferred_element_type=F32) * inv_root
            sc = jnp.where(seen, sc, -1e30)
            m = jnp.max(sc, axis=0, keepdims=True)
            e = jnp.where(seen, jnp.exp(sc - m), 0.0)
            ml[g, 0:1, :] = m
            ml[g, 1:2, :] = jnp.sum(e, axis=0, keepdims=True)
            ol[g] = jnp.dot(vt[g], e.astype(BF16), preferred_element_type=F32)

    def merge(parts):
        top = functools.reduce(jnp.maximum, [m for m, _, _ in parts])
        e = [jnp.exp(m - top) for m, _, _ in parts]
        l = sum(a * b for a, (_, b, _) in zip(e, parts))
        o = sum(a * b for a, (_, _, b) in zip(e, parts))
        return top, l, o

    def held(side, g):
        c = slice(side * width, (side + 1) * width)
        return ml[g, 0:1, c], ml[g, 1:2, c], ol[g, :, c]

    def came(side, s, g):
        return rst[side, s, g, 0:1, :], rst[side, s, g, 1:2, :], ro[side, s, g].astype(F32)

    hh = heads // 2
    halves = (range(0, hh), range(hh, heads))
    osteps = []
    for s in range(half):
        d = half - s
        attend(at(d), p if s == 0 else at(-d))
        if s == 0:
            for g in range(heads):
                m, l, o = held(1, g)
                own_ml[g, 0:1, :] = m
                own_ml[g, 1:2, :] = l
                own_o[g] = o
        else:
            for c in osteps[s - 1]:
                c.wait_recv()
        step = []
        for side in range(2):
            todo = halves[side] if s == 0 else range(heads)
            for g in todo:
                parts = [held(0 if s == 0 else side, g)]
                if s > 1 or (s == 1 and g in halves[side]):
                    parts.append(came(side, s - 1, g))
                m, l, o = merge(parts) if len(parts) > 1 else parts[0]
                sst[side, s, g, 0:1, :] = m
                sst[side, s, g, 1:2, :] = l
                so[side, s, g] = o.astype(BF16)
            sel = pl.ds(todo[0], len(todo))
            for src, dst, a, b in ((so, ro, osend, orecv), (sst, rst, tsend, trecv)):
                step.append(
                    pltpu.make_async_remote_copy(
                        src.at[side, s, sel], dst.at[side, s, sel], a.at[side, s], b.at[side, s],
                        device_id={"pool": at(1 - 2 * side)}, device_id_type=MESH,
                    )
                )
        for c in step:
            c.start()
        osteps.append(step)
        if s + 1 < n - 1:
            ksends[s + 1].start()
    for c in osteps[half - 1]:
        c.wait_recv()
    for g in range(heads):
        parts = [
            (own_ml[g, 0:1, :], own_ml[g, 1:2, :], own_o[g]),
            came(0, half - 1, g),
            came(1, half - 1, g),
        ]
        _, l, o = merge(parts)
        att[p, g] = (o / l).T.astype(BF16)

    aring = [ring(att, asend, arecv, s) for s in range(half)]
    for s in range(half + 1):
        advance(aring, s)
        if s < half and half + s + 1 < n - 1:
            ksends[half + s + 1].start()

    for g in range(heads):
        planes = [att[c, g].astype(F32) for c in range(n)]
        for j in range(group):
            amat[:, (g * group + j) * HEAD : (g * group + j + 1) * HEAD] = jnp.concatenate(
                [v[j * rows : (j + 1) * rows] for v in planes], axis=0
            ).astype(BF16)
    oc.wait()
    oh = wo.shape[1] // 2

    def project(which, dst):
        @pl.loop(0, oh // cols)
        def _(i):
            src = pl.ds(pl.multiple_of(which * oh + i * cols, cols), cols)
            dst[:, pl.ds(pl.multiple_of(i * cols, cols), cols)] = jnp.dot(
                amat[...], wo[:, src], preferred_element_type=F32
            )

    project(other, psend)
    pcopy = pltpu.make_async_remote_copy(
        psend, precv, psem.at[0], psem.at[1], device_id={"tp": other}, device_id_type=MESH
    )
    pcopy.start()
    mine = [
        jnp.dot(
            amat[...],
            wo[:, pl.ds(pl.multiple_of(t * oh + i * cols, cols), cols)],
            preferred_element_type=F32,
        )
        for i in range(oh // cols)
    ]
    pcopy.wait_recv()
    for i, v in enumerate(mine):
        cc = slice(i * cols, (i + 1) * cols)
        ans[:, cc] = (v + precv[:, cc]).astype(BF16)

    for c in ksends:
        c.wait_recv()

    @pl.loop(0, 2 * kvw // cols)
    def _(i):
        cc = pl.ds(pl.multiple_of(i * cols, cols), cols)
        kv_out[:, cc] = jnp.dot(
            onehot_in[...], recvb[:, :, cc].reshape(moved, cols), preferred_element_type=F32
        ).astype(BF16)

    for c in dex + ksends + [pcopy]:
        c.wait_send()
    for s in range(half):
        for c in (*qring[s], *osteps[s], *aring[s]):
            c.wait_send()


def shards(doc_hidden, key_projector, value_projector, queries, lengths, page_slots, out_weight):
    n = lax.axis_size("pool")
    tokens, feat = doc_hidden.shape
    kvw = key_projector.shape[1]
    heads = kvw // HEAD
    rows = queries.shape[0]
    group = queries.shape[1] // kvw
    per = page_slots.shape[0] // n
    page = tokens // per
    cap = per // n + 1
    width = group * rows
    half = n // 2
    nb = 2
    oc = out_weight.shape[1]
    moved = cap * page
    any_spec = pl.BlockSpec(memory_space=pl.ANY)
    vmem = pl.BlockSpec(memory_space=pltpu.VMEM)
    dma = pltpu.SemaphoreType.DMA
    kv, ans = pl.pallas_call(
        functools.partial(kernel, n, rows, group, page, per, cap),
        out_shape=(
            jax.ShapeDtypeStruct((tokens, 2 * kvw), BF16),
            jax.ShapeDtypeStruct((n * rows, oc // 2), BF16),
        ),
        in_specs=[any_spec, any_spec, any_spec, vmem, vmem, vmem, any_spec],
        out_specs=(vmem, vmem),
        scratch_shapes=[
            pltpu.VMEM((2, tokens, feat), BF16),
            pltpu.VMEM((2 * feat, 2 * kvw), BF16),
            pltpu.VMEM(out_weight.shape, BF16),
            pltpu.VMEM((n, heads, width, HEAD), BF16),
            pltpu.VMEM((per, page, 2 * kvw), BF16),
            pltpu.VMEM((heads, HEAD, tokens), BF16),
            pltpu.VMEM((tokens, n * moved), BF16),
            pltpu.VMEM((n, moved, 2 * kvw), BF16),
            pltpu.VMEM((n, moved, 2 * kvw), BF16),
            pltpu.VMEM((heads, HEAD, 2 * width), F32),
            pltpu.VMEM((heads, 8, 2 * width), F32),
            pltpu.VMEM((heads, HEAD, width), F32),
            pltpu.VMEM((heads, 8, width), F32),
            pltpu.VMEM((2, half, heads, HEAD, width), BF16),
            pltpu.VMEM((2, half, heads, 8, width), F32),
            pltpu.VMEM((2, half, heads, HEAD, width), BF16),
            pltpu.VMEM((2, half, heads, 8, width), F32),
            pltpu.VMEM((n, heads, width, HEAD), BF16),
            pltpu.VMEM((n * rows, out_weight.shape[0]), BF16),
            pltpu.VMEM((n * rows, oc // 2), F32),
            pltpu.VMEM((n * rows, oc // 2), F32),
            dma((nb + 3,)), dma((nb,)), dma((nb,)),
            dma((2, half)), dma((2, half)), dma((2, half)), dma((2, half)),
            dma((n - 1,)), dma((n - 1,)),
            dma((2, half)), dma((2, half)), dma((2, half)), dma((2, half)),
            dma((2,)),
        ],
        compiler_params=pltpu.CompilerParams(
            collective_id=0, has_side_effects=True, vmem_limit_bytes=60 * 1024 * 1024
        ),
    )(
        doc_hidden, key_projector, value_projector, queries,
        lengths.reshape(1, -1), page_slots.reshape(1, -1), out_weight,
    )
    return kv.reshape(tokens, 2, kvw), ans


def solution(mesh):
    in_specs = (
        P(("rep", "pool"), "tp"),
        P(None, "tp"),
        P(None, "tp"),
        P(("rep", "pool"), "tp"),
        P("rep"),
        P("rep"),
        P("tp", "pool"),
    )
    out_specs = (P(("rep", "pool"), None, "tp"), P("rep", ("pool", "tp")))
    return jax.shard_map(shards, mesh=mesh, in_specs=in_specs, out_specs=out_specs, check_vma=False)
```

time: 266 us -> 108 us (0.41)
  waiting for transfers between devices: 164 us -> 0 us
  Pallas kernels: 0 us -> 102 us
  local copies, waits for them, and re-layouts: 30.7 us -> 4.19 us
  matrix products: 24.2 us -> 0 us
  starting transfers between devices: 18.5 us -> 0 us
  between operations: 15.8 us -> 0.64 us
  other arithmetic: 11.7 us -> 0 us
    all_gather x3 -> x0, waiting for transfers between devices: 111 us -> none  [the longest x1 48.8 us: shards(): query_all = lax.all_gather(queries, 'pool', axis=0, tiled=True)]
    pallas_call x0 -> x1, Pallas kernels: none -> 102 us  [shards(): pl.pallas_call(functools.partial(kernel, n, rows, group, page, per, cap),...]
    all_to_all x4 -> x0, waiting for transfers between devices: 47.4 us -> none  [the longest x1 43.5 us: shards(): lax.all_to_all(weighted[None], 'pool', split_axis=1, concat_axis=0, tiled...]
    dot_general x5 -> x0, matrix products: 24.2 us -> none  [the longest x1 7.3 us: shards(): jnp.dot(normed, value_projector, preferred_element_type=jnp.float32)]
    all_to_all x4 -> x0, starting transfers between devices: 18.4 us -> none  [the longest x1 5.93 us: shards(): lax.all_to_all(weighted[None], 'pool', split_axis=1, concat_axis=0, tiled...]
    scatter x5 -> x0, local copies, waits for them, and re-layouts: 12.7 us -> none  [the longest x2 5.13 us: shards(): cache_blocks = jnp.zeros((per_device, page_len, 2, kv_width), jnp.bfloat1...]
    reduce_sum x5 -> x0, other arithmetic: 8.12 us -> none  [the longest x1 5.25 us: shards(): jnp.mean(hidden * hidden, axis=-1, keepdims=True) + 1e-06]
    unnamed x19 -> x1, local copies, waits for them, and re-layouts: 8.7 us -> 1.57 us
  transfers between devices with their start and end apart: 8 -> 0, of which waited for: 6 -> 0; matrix products, arithmetic and copies ran while one was open for 7% -> 0% of each run, Pallas kernels for 0% -> 0%
where the time goes in v1:
time: 108 us; the launch traced here: 107 us
  Pallas kernels  102 us (94%)
  local copies, waits for them, and re-layouts  4.19 us (4%)
    pallas_call x1, Pallas kernels, shards(): pl.pallas_call(functools.partial(kernel, n, rows, group, page, per, cap),...  102 us
    reshape x1, local copies, waits for them, and re-layouts, shards(): return (kv.reshape(tokens, 2, kvw), ans)  2.62 us

profile of v1, /device:TPU:0, one launch (start us, length us, event | category | flops | bytes accessed | tf_op | source)
XLA Modules:
  0.0 107.1 jit_solution(1349050278260676275)
XLA Ops:
  0.6 102.2 %shard_map.86 = (bf16[512,1024]{1,0:T(8,128)(2,1)}, bf16[128,512]{1,0:T(8,128)(2,1)}) custom-call(bf16[512,4096]{1,0:T(8,128)(2,1)} %doc.1, bf16[8192,512]{1,0:T(8,128)(2,1)} %wk.1, bf16[8192,512]{1,0:T(8,128)(2,1)} %wv.1, bf16[16,4096]{1,0:T(8,128)(2,1)} %q.1, s32[1,128]{1,0:T(1,128)} %bitcast.3, s32[1,256]{1,0:T(1,128)} %bitcast.2, bf16[4096,1024]{1,0:T(8,128)(2,1)} %ow.1), custom_call_target="tpu_custom_call" | custom-call | tf_op jit(solution)/shard_map/pallas_call | solution.py:383
  102.9 2.6 %reshape.15 = bf16[512,2,512]{2,1,0:T(2,128)(2,1)} reshape(bf16[512,1024]{1,0:T(8,128)(2,1)} %get-tuple-element.4) | data formatting | bytes 2097152 | tf_op jit(solution)/shard_map/reshape | solution.py:426
  105.5 1.6 %copy.10 = bf16[128,512]{1,0:T(8,128)(2,1)} copy(bf16[128,512]{1,0:T(8,128)(2,1)} %get-tuple-element.9) | data formatting | bytes 262144

commit v2 on v1

--- a/solution.py
+++ b/solution.py
@@ -87,33 +87,32 @@
     ]
     for c in dex:
         c.start()
-    oc.start()
+
+    hh = heads // 2
+    halves = (range(0, hh), range(hh, heads))
 
     def ring(buf, ssem, rsem, s):
-        hh = heads // 2
-        a, b = at(-s), at(s)
-        if s == half - 1:
-            ra, rb = buf.at[a, pl.ds(0, hh)], buf.at[b, pl.ds(hh, heads - hh)]
-        else:
-            ra, rb = buf.at[a], buf.at[b]
-        return (
-            pltpu.make_async_remote_copy(
-                ra, ra, ssem.at[0, s], rsem.at[0, s],
-                device_id={"pool": at(1)}, device_id_type=MESH,
-            ),
-            pltpu.make_async_remote_copy(
-                rb, rb, ssem.at[1, s], rsem.at[1, s],
-                device_id={"pool": at(-1)}, device_id_type=MESH,
-            ),
-        )
+        return {
+            (side, g): pltpu.make_async_remote_copy(
+                buf.at[at(s * (2 * side - 1)), g], buf.at[at(s * (2 * side - 1)), g],
+                ssem.at[side, s, g], rsem.at[side, s, g],
+                device_id={"pool": at(1 - 2 * side)}, device_id_type=MESH,
+            )
+            for g in range(heads)
+            for side in range(2)
+            if s < half - 1 or g in halves[side]
+        }
+
+    def order(side, g):
+        return (g, side) if side == 0 else (heads - 1 - g, side)
 
     def advance(steps, s):
-        if s > 0:
-            for c in steps[s - 1]:
-                c.wait_recv()
-        if s < half:
-            for c in steps[s]:
-                c.start()
+        keys = sorted(steps[min(s, half - 1)] if s == 0 else steps[s - 1], key=lambda k: order(*k))
+        for k in keys:
+            if s > 0:
+                steps[s - 1][k].wait_recv()
+            if s < half and k in steps[s]:
+                steps[s][k].start()
 
     qring = [ring(qall, qsend, qrecv, s) for s in range(half)]
     advance(qring, 0)
@@ -146,41 +145,63 @@
 
     feat = x.shape[2]
     cols = 256
-    qstep = 1
-    for b in range(nb):
-        dloc[b].wait()
-        dex[b].wait_recv()
-
-        @pl.loop(0, brows // 16)
-        def _(i):
-            r = pl.ds(pl.multiple_of(b * brows + i * 16, 16), 16)
-            ss = jnp.zeros((16, 1), F32)
-            for h in range(2):
-                v = x[h, r, :].astype(F32)
-                ss = ss + jnp.sum(v * v, axis=-1, keepdims=True)
-            scale = lax.rsqrt(ss / (2 * feat) + 1e-06)
-            for h in range(2):
-                x[h, r, :] = (x[h, r, :].astype(F32) * scale).astype(BF16)
-
-        if qstep < half:
-            advance(qring, qstep)
-            qstep += 1
-        if b == 0:
-            for c in wc:
-                c.wait()
-
-        @pl.loop(0, 2 * kvw // cols)
-        def _(i):
-            cc = pl.ds(pl.multiple_of(i * cols, cols), cols)
-            acc = jnp.dot(x[0, blk(b), :], w[pl.ds(0, feat), cc], preferred_element_type=F32)
-            acc += jnp.dot(x[1, blk(b), :], w[pl.ds(feat, feat), cc], preferred_element_type=F32)
-            kvb[pl.ds(b * brows // page, brows // page), :, cc] = acc.astype(BF16).reshape(
-                brows // page, page, cols
-            )
-
-        if qstep < half:
-            advance(qring, qstep)
-            qstep += 1
+    nsub = 2 * kvw // cols
+
+    def norm(r):
+        ss = jnp.zeros((16, 1), F32)
+        for h in range(2):
+            v = x[h, r, :].astype(F32)
+            ss = ss + jnp.sum(v * v, axis=-1, keepdims=True)
+        scale = lax.rsqrt(ss / (2 * feat) + 1e-06)
+        for h in range(2):
+            x[h, r, :] = (x[h, r, :].astype(F32) * scale).astype(BF16)
+
+    def multiply(b, i):
+        cc = pl.ds(pl.multiple_of(i * cols, cols), cols)
+        acc = jnp.dot(x[0, blk(b), :], w[pl.ds(0, feat), cc], preferred_element_type=F32)
+        acc += jnp.dot(x[1, blk(b), :], w[pl.ds(feat, feat), cc], preferred_element_type=F32)
+        kvb[pl.ds(b * brows // page, brows // page), :, cc] = acc.astype(BF16).reshape(
+            brows // page, page, cols
+        )
+
+    dloc[0].wait()
+    dex[0].wait_recv()
+
+    @pl.loop(0, brows // 16)
+    def _(i):
+        norm(pl.ds(pl.multiple_of(i * 16, 16), 16))
+
+    advance(qring, 1)
+    wc[0].wait()
+    dloc[1].wait()
+    dex[1].wait_recv()
+    each = brows // 16 // (kvw // cols)
+
+    @pl.loop(0, kvw // cols)
+    def _(i):
+        multiply(0, i)
+        for e in range(each):
+            norm(pl.ds(pl.multiple_of(brows + (i * each + e) * 16, 16), 16))
+
+    wc[1].wait()
+    oc.start()
+    qstep = 2
+    if half >= qstep:
+        advance(qring, qstep)
+        qstep += 1
+
+    @pl.loop(0, kvw // cols)
+    def _(i):
+        multiply(1, i)
+
+    if half >= qstep:
+        advance(qring, qstep)
+        qstep += 1
+
+    @pl.loop(kvw // cols, nsub)
+    def _(i):
+        multiply(0, i)
+        multiply(1, i)
 
     onehot_out = jnp.where(iota((moved, tokens), 0) == drow, 1.0, 0.0).astype(BF16)
 
@@ -201,7 +222,13 @@
         )
         for k in range(1, n)
     ]
-    ksends[0].start()
+
+    def kv_start(step):
+        turns = {0: (0, n - 2), half: (1, n - 3), 2 * half: range(2, n - 3)}
+        for i in turns.get(step, ()):
+            ksends[i].start()
+
+    kv_start(0)
 
     while qstep <= half:
         advance(qring, qstep)
@@ -240,22 +267,13 @@
             ml[g, 1:2, :] = jnp.sum(e, axis=0, keepdims=True)
             ol[g] = jnp.dot(vt[g], e.astype(BF16), preferred_element_type=F32)
 
-    def merge(parts):
-        top = functools.reduce(jnp.maximum, [m for m, _, _ in parts])
-        e = [jnp.exp(m - top) for m, _, _ in parts]
-        l = sum(a * b for a, (_, b, _) in zip(e, parts))
-        o = sum(a * b for a, (_, _, b) in zip(e, parts))
-        return top, l, o
-
     def held(side, g):
         c = slice(side * width, (side + 1) * width)
         return ml[g, 0:1, c], ml[g, 1:2, c], ol[g, :, c]
 
-    def came(side, s, g):
-        return rst[side, s, g, 0:1, :], rst[side, s, g, 1:2, :], ro[side, s, g].astype(F32)
-
-    hh = heads // 2
-    halves = (range(0, hh), range(hh, heads))
+    def stats(side, s, g):
+        return rst[side, s, g : g + 1, :], rst[side, s, heads + g : heads + g + 1, :]
+
     osteps = []
     for s in range(half):
         d = half - s
@@ -263,52 +281,73 @@
         if s == 0:
             for g in range(heads):
                 m, l, o = held(1, g)
-                own_ml[g, 0:1, :] = m
-                own_ml[g, 1:2, :] = l
+                own_ml[g : g + 1, :] = m
+                own_ml[heads + g : heads + g + 1, :] = l
                 own_o[g] = o
-        else:
-            for c in osteps[s - 1]:
-                c.wait_recv()
-        step = []
+        step = {}
         for side in range(2):
-            todo = halves[side] if s == 0 else range(heads)
-            for g in todo:
-                parts = [held(0 if s == 0 else side, g)]
+            to = dict(device_id={"pool": at(1 - 2 * side)}, device_id_type=MESH)
+            step[side, -1] = pltpu.make_async_remote_copy(
+                sst.at[side, s], rst.at[side, s], tsend.at[side, s], trecv.at[side, s], **to
+            )
+            for g in range(heads):
+                if s > 0 or g in halves[side]:
+                    step[side, g] = pltpu.make_async_remote_copy(
+                        so.at[side, s, g], ro.at[side, s, g],
+                        osend.at[side, s, g], orecv.at[side, s, g], **to
+                    )
+        if s > 0:
+            for side in range(2):
+                osteps[s - 1][side, -1].wait_recv()
+        for side in range(2):
+            for g in range(heads):
+                m, l, _ = held(0 if s == 0 else side, g)
                 if s > 1 or (s == 1 and g in halves[side]):
-                    parts.append(came(side, s - 1, g))
-                m, l, o = merge(parts) if len(parts) > 1 else parts[0]
-                sst[side, s, g, 0:1, :] = m
-                sst[side, s, g, 1:2, :] = l
-                so[side, s, g] = o.astype(BF16)
-            sel = pl.ds(todo[0], len(todo))
-            for src, dst, a, b in ((so, ro, osend, orecv), (sst, rst, tsend, trecv)):
-                step.append(
-                    pltpu.make_async_remote_copy(
-                        src.at[side, s, sel], dst.at[side, s, sel], a.at[side, s], b.at[side, s],
-                        device_id={"pool": at(1 - 2 * side)}, device_id_type=MESH,
-                    )
-                )
-        for c in step:
-            c.start()
+                    m1, l1 = stats(side, s - 1, g)
+                    top = jnp.maximum(m, m1)
+                    l = l * jnp.exp(m - top) + l1 * jnp.exp(m1 - top)
+                    m = top
+                sst[side, s, g : g + 1, :] = m
+                sst[side, s, heads + g : heads + g + 1, :] = l
+            step[side, -1].start()
+        for side, g in sorted(
+            (k for k in step if k[1] >= 0), key=lambda k: (k[1] in halves[k[0]], order(*k))
+        ):
+            m, l, o = held(0 if s == 0 else side, g)
+            if s > 1 or (s == 1 and g in halves[side]):
+                osteps[s - 1][side, g].wait_recv()
+                m1, l1 = stats(side, s - 1, g)
+                top = jnp.maximum(m, m1)
+                o = o * jnp.exp(m - top) + ro[side, s - 1, g].astype(F32) * jnp.exp(m1 - top)
+            so[side, s, g] = o.astype(BF16)
+            step[side, g].start()
         osteps.append(step)
-        if s + 1 < n - 1:
-            ksends[s + 1].start()
-    for c in osteps[half - 1]:
-        c.wait_recv()
+        kv_start(s + 1)
+    for side in range(2):
+        osteps[half - 1][side, -1].wait_recv()
+    aring = [ring(att, asend, arecv, s) for s in range(half)]
     for g in range(heads):
-        parts = [
-            (own_ml[g, 0:1, :], own_ml[g, 1:2, :], own_o[g]),
-            came(0, half - 1, g),
-            came(1, half - 1, g),
-        ]
-        _, l, o = merge(parts)
+        ms = [own_ml[g : g + 1, :]]
+        ls = [own_ml[heads + g : heads + g + 1, :]]
+        os = [own_o[g]]
+        for side in range(2):
+            osteps[half - 1][side, g].wait_recv()
+            m1, l1 = stats(side, half - 1, g)
+            ms.append(m1)
+            ls.append(l1)
+            os.append(ro[side, half - 1, g].astype(F32))
+        top = functools.reduce(jnp.maximum, ms)
+        e = [jnp.exp(m - top) for m in ms]
+        l = sum(a * b for a, b in zip(e, ls))
+        o = sum(a * b for a, b in zip(e, os))
         att[p, g] = (o / l).T.astype(BF16)
-
-    aring = [ring(att, asend, arecv, s) for s in range(half)]
-    for s in range(half + 1):
+        for side in range(2):
+            if (side, g) in aring[0]:
+                aring[0][side, g].start()
+    kv_start(half + 1)
+    for s in range(1, half + 1):
         advance(aring, s)
-        if s < half and half + s + 1 < n - 1:
-            ksends[half + s + 1].start()
+        kv_start(half + s + 1)
 
     for g in range(heads):
         planes = [att[c, g].astype(F32) for c in range(n)]
@@ -358,7 +397,7 @@
     for c in dex + ksends + [pcopy]:
         c.wait_send()
     for s in range(half):
-        for c in (*qring[s], *osteps[s], *aring[s]):
+        for c in (*qring[s].values(), *osteps[s].values(), *aring[s].values()):
             c.wait_send()
 
 
@@ -401,19 +440,20 @@
             pltpu.VMEM((heads, HEAD, 2 * width), F32),
             pltpu.VMEM((heads, 8, 2 * width), F32),
             pltpu.VMEM((heads, HEAD, width), F32),
-            pltpu.VMEM((heads, 8, width), F32),
+            pltpu.VMEM((2 * heads, width), F32),
             pltpu.VMEM((2, half, heads, HEAD, width), BF16),
-            pltpu.VMEM((2, half, heads, 8, width), F32),
+            pltpu.VMEM((2, half, 2 * heads, width), F32),
             pltpu.VMEM((2, half, heads, HEAD, width), BF16),
-            pltpu.VMEM((2, half, heads, 8, width), F32),
+            pltpu.VMEM((2, half, 2 * heads, width), F32),
             pltpu.VMEM((n, heads, width, HEAD), BF16),
             pltpu.VMEM((n * rows, out_weight.shape[0]), BF16),
             pltpu.VMEM((n * rows, oc // 2), F32),
             pltpu.VMEM((n * rows, oc // 2), F32),
             dma((nb + 3,)), dma((nb,)), dma((nb,)),
-            dma((2, half)), dma((2, half)), dma((2, half)), dma((2, half)),
+            dma((2, half, heads)), dma((2, half, heads)),
+            dma((2, half, heads)), dma((2, half, heads)),
             dma((n - 1,)), dma((n - 1,)),
-            dma((2, half)), dma((2, half)), dma((2, half)), dma((2, half)),
+            dma((2, half, heads)), dma((2, half, heads)), dma((2, half)), dma((2, half)),
             dma((2,)),
         ],
         compiler_params=pltpu.CompilerParams(

time: 108 us -> 91.2 us (0.84)
  Pallas kernels: 102 us -> 86.2 us
    pallas_call x1, Pallas kernels: 102 us -> 86.2 us  [shards(): pl.pallas_call(functools.partial(kernel, n, rows, group, page, per, cap),...]
where the time goes in v2:
time: 91.2 us; the launch traced here: 91 us
  Pallas kernels  86.2 us (95%)
  local copies, waits for them, and re-layouts  4.19 us (5%)
    pallas_call x1, Pallas kernels, shards(): pl.pallas_call(functools.partial(kernel, n, rows, group, page, per, cap),...  86.2 us
    reshape x1, local copies, waits for them, and re-layouts, shards(): return (kv.reshape(tokens, 2, kvw), ans)  2.62 us

profile of v2, /device:TPU:0, one launch (start us, length us, event | category | flops | bytes accessed | tf_op | source)
XLA Modules:
  0.0 91.0 jit_solution(9919742642275302274)
XLA Ops:
  0.6 86.2 %shard_map.86 = (bf16[512,1024]{1,0:T(8,128)(2,1)}, bf16[128,512]{1,0:T(8,128)(2,1)}) custom-call(bf16[512,4096]{1,0:T(8,128)(2,1)} %doc.1, bf16[8192,512]{1,0:T(8,128)(2,1)} %wk.1, bf16[8192,512]{1,0:T(8,128)(2,1)} %wv.1, bf16[16,4096]{1,0:T(8,128)(2,1)} %q.1, s32[1,128]{1,0:T(1,128)} %bitcast.3, s32[1,256]{1,0:T(1,128)} %bitcast.2, bf16[4096,1024]{1,0:T(8,128)(2,1)} %ow.1), custom_call_target="tpu_custom_call" | custom-call | tf_op jit(solution)/shard_map/pallas_call | solution.py:422
  86.8 2.6 %reshape.15 = bf16[512,2,512]{2,1,0:T(2,128)(2,1)} reshape(bf16[512,1024]{1,0:T(8,128)(2,1)} %get-tuple-element.4) | data formatting | bytes 2097152 | tf_op jit(solution)/shard_map/reshape | solution.py:466
  89.4 1.6 %copy.10 = bf16[128,512]{1,0:T(8,128)(2,1)} copy(bf16[128,512]{1,0:T(8,128)(2,1)} %get-tuple-element.9) | data formatting | bytes 262144
